TPU v7x, 512 devices: a whole 4x4x16 slice. The times are simulated.
512 devices in a mesh: section: 8 (over z_hi, core), dp: 16 (over y, z_lo), mp: 4 (over x).
Axes of the slice: x: 4, y: 4, z: 16 (z_hi: 4, z_lo: 4; z = z_hi * 4 + z_lo), core: 2. Of those that a mesh axis runs over, the one named last changes fastest.
Arguments:
- activations: bfloat16 [8, 4096, 8192], P('section', 'dp', 'mp'), may hold values from -6 to 6
- value_gradient: bfloat16 [8, 4096, 1024], P('section', 'dp', 'mp'), may hold values from -6 to 6
- value_matrix: bfloat16 [8, 8192, 1024], P('section', ('mp', 'dp')), may hold values from -0.1875 to 0.1875
- adapter_down_weight: bfloat16 [8, 16, 32, 8192], P('section', 'dp', None, 'mp'), may hold values from -0.0625 to 0.0625
- adapter_up_weight: bfloat16 [8, 16, 32, 1024], P('section', 'dp', None, 'mp'), may hold values from -0.1875 to 0.1875
- segment_adapter: int32 [8, 32], P('section', 'dp'), may hold values from 0 to 15
- adapter_slot: int32 [16], replicated, may hold values from 0 to 15, each once
Outputs:
- received: bfloat16 [8, 4096, 8192], P('section', 'dp', 'mp')
- down_gradient: bfloat16 [8, 16, 32, 8192], P('section', 'dp', None, 'mp')
- up_gradient: bfloat16 [8, 16, 32, 1024], P('section', 'dp', None, 'mp')
Inputs may be any that keep to these rules, and one draw needn't show every extreme that they name: adapter_slot is a permutation of the adapters.
All inputs are finite; a program needn't handle non-finite values.
Results may differ from a plain program's by a relative error of at most 0.025.
Values may be sent and summed in bfloat16 or wider, within the bound.
A program may use at most 64 MiB of HBM per device.

v0:
```python
import math

import jax
import jax.numpy as jnp
from jax import lax
from jax.sharding import PartitionSpec as P

ADAPTERS_PER_DP = 1


ADAPTER_SCALE = 2.0


def passed_along(block, axis, distance):
    devices = range(lax.axis_size(axis))
    route = [((i - distance) % len(devices), i) for i in devices]
    return lax.ppermute(block, axis, route)


def select_rows(picker, table):
    flat_table = table.reshape(table.shape[0], -1)
    chosen = jnp.dot(picker, flat_table, preferred_element_type=jnp.float32)
    return chosen.astype(jnp.bfloat16).reshape((picker.shape[0],) + table.shape[1:])


def body(
    activations,
    value_gradient,
    value_matrix,
    adapter_down_weight,
    adapter_up_weight,
    segment_adapter,
    adapter_slot,
):
    tokens_here = activations[0]
    grad_here = value_gradient[0]
    row_total = tokens_here.shape[0]
    local_width = tokens_here.shape[1]
    seg_ids = segment_adapter[0]
    segments_here = seg_ids.shape[0]
    seg_rows = row_total // segments_here
    full_grad = lax.all_gather(grad_here, "mp", axis=1, tiled=True)
    frozen_term = jnp.einsum(
        "tv,kv->tk",
        full_grad,
        lax.all_gather(value_matrix[0], "dp", axis=0, tiled=True),
        preferred_element_type=jnp.float32,
    )
    down_all, up_all = (
        lax.all_gather(adapter_down_weight[0], "dp", axis=0, tiled=True),
        lax.all_gather(adapter_up_weight[0], "dp", axis=0, tiled=True),
    )
    adapter_number = down_all.shape[0]
    rank_size = down_all.shape[1]
    adapter_labels = jnp.arange(adapter_number, dtype=jnp.int32)
    adapter_hits = (seg_ids[:, None] == adapter_labels[None, :]).astype(jnp.int32)
    slot_position = jnp.sum(adapter_hits * adapter_slot[None, :], axis=1)
    picker = (slot_position[:, None] == adapter_labels[None, :]).astype(jnp.bfloat16)
    down_segment = select_rows(picker, down_all)
    token_seg = tokens_here.reshape(segments_here, seg_rows, local_width)
    grad_seg = grad_here.reshape(segments_here, seg_rows, grad_here.shape[1])
    hidden_part = jnp.einsum(
        "ksd,krd->ksr", token_seg, down_segment, preferred_element_type=jnp.float32
    ).reshape(-1, 128)
    up_segment = select_rows(picker, up_all)
    grad_part = jnp.einsum(
        "ksv,krv->ksr", grad_seg, up_segment, preferred_element_type=jnp.float32
    ).reshape(-1, 128)
    hidden_sum, grad_sum = (
        lax.psum(hidden_part.astype(jnp.bfloat16), "mp").astype(jnp.float32),
        lax.psum(grad_part.astype(jnp.bfloat16), "mp").astype(jnp.float32),
    )
    rank_gradient = grad_sum.reshape(segments_here, seg_rows, rank_size).astype(jnp.bfloat16)
    hidden = hidden_sum.reshape(segments_here, seg_rows, rank_size).astype(jnp.bfloat16)
    adapter_term = jnp.einsum(
        "xcf,xfv->xcv", rank_gradient, down_segment, preferred_element_type=jnp.float32
    ).reshape(row_total, local_width)
    input_gradient = (frozen_term + ADAPTER_SCALE * adapter_term).astype(jnp.bfloat16)
    received = passed_along(input_gradient, "section", -1)
    gradient_norm = ADAPTER_SCALE / math.sqrt(row_total / ADAPTERS_PER_DP)
    part_down = jnp.einsum(
        "ksr,ksd->krd", rank_gradient, token_seg, preferred_element_type=jnp.float32
    )
    partial_up = jnp.einsum("ksr,ksv->krv", hidden, grad_seg, preferred_element_type=jnp.float32)
    select_float = picker.astype(jnp.float32)
    slot_down = (
        jnp.einsum("ka,krd->ard", select_float, part_down, precision=lax.Precision.HIGHEST)
        * gradient_norm
    )
    slot_up = (
        jnp.einsum("lh,lzn->hzn", select_float, partial_up, precision=lax.Precision.HIGHEST)
        * gradient_norm
    )
    down_gradient, up_gradient = (
        lax.psum_scatter(
            slot_down.astype(jnp.bfloat16), "dp", scatter_dimension=0, tiled=True
        ).astype(jnp.float32),
        lax.psum_scatter(
            slot_up.astype(jnp.bfloat16), "dp", scatter_dimension=0, tiled=True
        ).astype(jnp.float32),
    )
    return (
        received[None],
        down_gradient.astype(jnp.bfloat16)[None],
        up_gradient.astype(jnp.bfloat16)[None],
    )


def solution(mesh):
    placed = (
        P("section", "dp", "mp"),
        P("section", "dp", "mp"),
        P("section", ("mp", "dp"), None),
        P("section", "dp", None, "mp"),
        P("section", "dp", None, "mp"),
        P("section", "dp"),
        P(),
    )
    return jax.shard_map(
        body,
        mesh=mesh,
        in_specs=placed,
        out_specs=(
            P("section", "dp", "mp"),
            P("section", "dp", None, "mp"),
            P("section", "dp", None, "mp"),
        ),
        check_vma=False,
    )
```

profile of v0, /device:TPU:4, one launch (start us, length us, event | category | flops | bytes accessed | tf_op | source)
XLA Modules:
  0.0 432.0 jit_solution(3788380156216784015)
XLA Ops:
  7.2 0.0 copy-start
  7.2 0.0 all-gather.9.cloned.1.call-start
  7.2 0.7 all-gather.9.cloned.1.call-update
  7.9 0.0 all-gather.7.cloned.1.call-start
  8.0 0.7 all-gather.7.cloned.1.call-update
  8.7 0.0 reduce-scatter.5.cloned.1.call-start
  8.7 46.9 %all-gather.2 = bf16[16,1,32,256]{3,2,1,0:T(8,128)(2,1)S(1)} all-gather(bf16[1,1,32,256]{3,2,1,0:T(8,128)(2,1)} %param.11), channel_id=4, replica_groups=mesh['section'=8,'dp'=16,'mp'=4] {'dp'}, dimensions={0}, use_global_device_ids=true | all-gather | bytes 278528 | tf_op jit(solution)/shard_map/all_gather | solution.py:51
  55.6 0.1 copy.18
  55.8 0.9 fusion.22
  56.6 0.2 convolution_convert_fusion.1
  56.9 1.0 fusion.9
  57.9 49.3 %all-gather.9.cloned.1.call-done = bf16[16,1,32,2048]{3,2,1,0:T(8,128)(2,1)} async-done(((bf16[1,1,32,2048]{3,2,1,0:T(8,128)(2,1)}), bf16[16,1,32,2048]{3,2,1,0:T(8,128)(2,1)}) %all-gather.9.cloned.1.call-update) | async-done | bytes 2097168 | tf_op jit(solution)/shard_map/all_gather | solution.py:50
  107.2 2.7 copy.20
  110.0 0.0 copy-start.1
  110.0 0.5 convolution_convert_fusion
  110.5 0.0 copy-done
  110.5 0.5 fusion.10
  111.0 16.0 %all-reduce = (bf16[2,128,32]{1,2,0:T(8,128)(2,1)S(1)}, bf16[2,128,32]{1,2,0:T(8,128)(2,1)S(1)}) all-reduce(bf16[2,128,32]{1,2,0:T(8,128)(2,1)S(1)} %fusion.9, bf16[2,128,32]{1,2,0:T(8,128)(2,1)S(1)} %fusion.10), channel_id=1, replica_groups=mesh['section'=8,'dp'=16,'mp'=4] {'mp'}, use_global_device_ids=true, to_apply=%region_1.0 | all-reduce | flops 16384 | bytes 65536 | tf_op jit(solution)/shard_map/psum | solution.py:71
  127.0 0.0 copy-done.1
  127.0 0.1 fusion.28
  127.1 0.5 fusion.8
  127.7 0.8 copy.17
  128.5 0.0 reduce-scatter.5.cloned.1.call-update
  128.5 0.0 reduce-scatter.3.cloned.1.call-start
  128.5 0.3 fusion.27
  128.8 2.4 multiply_convert_fusion
  131.3 2.5 copy.15
  133.7 0.0 reduce-scatter.3.cloned.1.call-update
  133.8 13.5 %all-gather = bf16[1,256,1024]{2,1,0:T(8,128)(2,1)} all-gather(bf16[1,256,256]{2,1,0:T(8,128)(2,1)S(1)} %copy-done.1), channel_id=2, replica_groups=mesh['section'=8,'dp'=16,'mp'=4] {'mp'}, dimensions={2}, use_global_device_ids=true | all-gather | bytes 655360 | tf_op jit(solution)/shard_map/all_gather | solution.py:42
  147.3 0.5 convolution_multiply_fusion
  147.8 68.0 %all-gather.7.cloned.1.call-done = bf16[1,2048,1024]{2,1,0:T(8,128)(2,1)} async-done(((bf16[1,128,1024]{2,1,0:T(8,128)(2,1)}), bf16[1,2048,1024]{2,1,0:T(8,128)(2,1)}) %all-gather.7.cloned.1.call-update) | async-done | bytes 4194320 | tf_op jit(solution)/shard_map/all_gather | solution.py:46
  215.8 3.6 fusion.5
  219.5 4.9 %collective-permute-start = (bf16[256,2048]{1,0:T(8,128)(2,1)S(1)}, bf16[256,2048]{1,0:T(8,128)(2,1)S(1)}, u32[]{:S(2)}, u32[]{:S(2)}) collective-permute-start(bf16[256,2048]{1,0:T(8,128)(2,1)S(1)} %fusion.5), channel_id=1, source_target_pairs={{64,0},{128,64},{192,128},{256,192},{320,256},{384,320},{448,384},... | collective-permute-start | bytes 3145736 | tf_op jit(solution)/shard_map/ppermute | solution.py:17
  224.4 39.9 %collective-permute-done = bf16[256,2048]{1,0:T(8,128)(2,1)S(1)} collective-permute-done((bf16[256,2048]{1,0:T(8,128)(2,1)S(1)}, bf16[256,2048]{1,0:T(8,128)(2,1)S(1)}, u32[]{:S(2)}, u32[]{:S(2)}) %collective-permute-start) | collective-permute-done | bytes 1048608 | tf_op jit(solution)/shard_map/ppermute | solution.py:17
  264.2 58.1 %reduce-scatter.5.cloned.1.call-done = bf16[1,32,256]{2,1,0:T(8,128)(2,1)} async-done(((bf16[16,32,256]{2,1,0:T(8,128)(2,1)}), bf16[1,32,256]{2,1,0:T(8,128)(2,1)}) %reduce-scatter.5.cloned.1.call-update) | async-done | bytes 16400 | tf_op jit(solution)/shard_map/reduce_scatter | solution.py:98
  322.4 102.1 %reduce-scatter.3.cloned.1.call-done = bf16[1,32,2048]{2,1,0:T(8,128)(2,1)} async-done(((bf16[16,32,2048]{2,1,0:T(8,128)(2,1)}), bf16[1,32,2048]{2,1,0:T(8,128)(2,1)}) %reduce-scatter.3.cloned.1.call-update) | async-done | bytes 131088 | tf_op jit(solution)/shard_map/reduce_scatter | solution.py:95
  424.5 1.0 copy.39
Async XLA Ops:
  7.2 103.3 %copy-start = (bf16[1,256,2048]{2,1,0:T(8,128)(2,1)S(1)}, bf16[1,256,2048]{2,1,0:T(8,128)(2,1)}, u32[]{:S(2)}) copy-start(bf16[1,256,2048]{2,1,0:T(8,128)(2,1)} %param.7) | copy-start | bytes 3145732
  7.2 100.1 %all-gather.9.cloned.1.call-start = ((), (), s32[]{:S(2)}) async-start(), calls=%async_computation.5 | async-start | bytes 2228224 | tf_op jit(solution)/shard_map/all_gather | solution.py:50
  7.9 207.9 %all-gather.7.cloned.1.call-start = ((), (), s32[]{:S(2)}) async-start(), calls=%async_computation.4 | async-start | bytes 4456448 | tf_op jit(solution)/shard_map/all_gather | solution.py:46
  8.7 313.7 %reduce-scatter.5.cloned.1.call-start = ((), (), s32[]{:S(2)}) async-start(), calls=%async_computation.3 | async-start | bytes 278528 | tf_op jit(solution)/shard_map/reduce_scatter | solution.py:98
  110.0 17.0 %copy-start.1 = (bf16[1,256,256]{2,1,0:T(8,128)(2,1)S(1)}, bf16[1,256,256]{2,1,0:T(8,128)(2,1)}, u32[]{:S(2)}) copy-start(bf16[1,256,256]{2,1,0:T(8,128)(2,1)} %param.8) | copy-start | bytes 393220
  128.5 296.0 %reduce-scatter.3.cloned.1.call-start = ((), (), s32[]{:S(2)}) async-start(), calls=%async_computation.2 | async-start | bytes 2228224 | tf_op jit(solution)/shard_map/reduce_scatter | solution.py:95
  219.5 44.8 %collective-permute-start = (bf16[256,2048]{1,0:T(8,128)(2,1)S(1)}, bf16[256,2048]{1,0:T(8,128)(2,1)S(1)}, u32[]{:S(2)}, u32[]{:S(2)}) collective-permute-start(bf16[256,2048]{1,0:T(8,128)(2,1)S(1)} %fusion.5), channel_id=1, source_target_pairs={{64,0},{128,64},{192,128},{256,192},{320,256},{384,320},{448,384},... | collective-permute-start | bytes 3145736 | tf_op jit(solution)/shard_map/ppermute | solution.py:17
Sparse Core Ops, SparseCore 0:
  10.1 97.1 all-gather.8
  109.3 106.4 all-gather.6
  219.2 103.1 reduce-scatter.4
  325.9 98.6 reduce-scatter.2
where the time goes:
time: 432 us
  waiting for transfers between devices  319 us (74%)
  blocking collectives  76.5 us (18%)
  between operations  13.8 us (3%)
  matrix products  9.72 us (2%)
  local copies, waits for them, and re-layouts  7.14 us (2%)
  starting transfers between devices  5.05 us (1%)
    reduce_scatter x1, waiting for transfers between devices, body(): lax.psum_scatter(slot_down.astype(jnp.bfloat16), 'dp', scatter_dimension=...  102 us
    all_gather x1, waiting for transfers between devices, body(): lax.all_gather(value_matrix[0], 'dp', axis=0, tiled=True)  68 us
    reduce_scatter x1, waiting for transfers between devices, body(): lax.psum_scatter(slot_up.astype(jnp.bfloat16), 'dp', scatter_dimension=0,...  58.1 us
    all_gather x1, waiting for transfers between devices, body(): lax.all_gather(adapter_down_weight[0], 'dp', axis=0, tiled=True)  49.3 us
    all_gather x1, blocking collectives, body(): lax.all_gather(adapter_up_weight[0], 'dp', axis=0, tiled=True)  46.9 us
    ppermute x1, waiting for transfers between devices, passed_along(): return lax.ppermute(block, axis, route)  39.9 us
    psum x1, blocking collectives, body(): lax.psum(grad_part.astype(jnp.bfloat16), 'mp').astype(jnp.float32)  16 us
    all_gather x1, blocking collectives, body(): full_grad = lax.all_gather(grad_here, 'mp', axis=1, tiled=True)  13.5 us
  transfers between devices with their start and end apart: 5, of which 5 were waited for; matrix products, arithmetic and copies ran while one was open for 4% of the time, Pallas kernels for 0%

commit v1 on v0

v1 whole, which is shorter than its diff:
```python
import functools
import math

import jax
import jax.numpy as jnp
from jax import lax
from jax.experimental import pallas as pl
from jax.experimental.pallas import tpu as pltpu
from jax.sharding import PartitionSpec as P

ADAPTERS_PER_DP = 1
ADAPTER_SCALE = 2.0
MESH = pl.DeviceIdType.MESH
BF16 = jnp.bfloat16
F32 = jnp.float32

NY = 4
NZ = 4
NX = 4
NS = 8


def nt_dot(a, b):
    return lax.dot_general(a, b, (((1,), (1,)), ((), ())), preferred_element_type=F32)


def nn_dot(a, b):
    return lax.dot_general(a, b, (((1,), (0,)), ((), ())), preferred_element_type=F32)


def tn_dot(a, b):
    return lax.dot_general(a, b, (((0,), (0,)), ((), ())), preferred_element_type=F32)


def kernel(
    act, grad, wmat, down, up, seg, slot,
    out, dgrad, ugrad,
    wn, gf, dns, dn, si, sin, uz, usel, ur, dz, dsel, dr,
    pm, rp, rr, rt, rtn, rx, hp, ht, pd, st, rsd, pu, su, rsu, ot,
    shift_s, w_r, w_s, g_r, g_sy, g_sx, dns_r, dna_r, dna_s, dnz_r, dnz_s,
    si_r, si_s, sin_r, sin_s, uz_r, uz_s, ur_r, ur_s, dz_r, dz_s, dr_r, dr_s,
    rp_r, rp_s, rtn_r, rtn_s, hp_r, hp_s, pd_r, pd_s, rsd_r, rsd_s,
    pu_r, pu_s, rsu_r, rsu_s, o_r, o_s,
):
    s = lax.axis_index("section")
    d = lax.axis_index("dp")
    x = lax.axis_index("mp")
    y, z = d // NZ, d % NZ
    first_core = s % 2 == 0
    before, after = (s + NS - 1) % NS, (s + 1) % NS
    rows = act.shape[0]
    seg_rows = rows // 2
    rank = down.shape[0]
    norm = ADAPTER_SCALE / math.sqrt(rows / ADAPTERS_PER_DP)

    def at(s_=s, y_=y, z_=z, x_=x):
        return {"section": s_, "dp": y_ * NZ + z_, "mp": x_}

    def copy(src, dst, ss, rs, device):
        return pltpu.make_async_remote_copy(
            src_ref=src, dst_ref=dst, send_sem=ss, recv_sem=rs,
            device_id=device, device_id_type=MESH,
        )

    def send(src, dst, ss, rs, device):
        copy(src, dst, ss, rs, device).start()

    def arrived(dst, rs):
        copy(dst, dst, rs, rs, at()).wait_recv()

    def sent(src, ss):
        copy(src, src, ss, ss, at()).wait_send()

    y_peers = [(y + k) % NY for k in (1, 3, 2)]
    x_peers = [(x + k) % NX for k in (1, 3, 2)]
    z_peers = [(z + k) % NZ for k in (1, 2, 3)]

    bar = pltpu.get_barrier_semaphore()
    peers = (
        [at(y_=p) for p in y_peers] + [at(x_=p) for p in x_peers] + [at(z_=p) for p in z_peers]
        + [at(s_=before, y_=k) for k in range(NY)] + [at(s_=after, y_=k) for k in range(NY)]
    )
    for p in peers:
        pl.semaphore_signal(bar, inc=1, device_id=p, device_id_type=MESH)
    pl.semaphore_wait(bar, len(peers))

    def line_out(buf, i, ss, rs, right, left):
        @pl.when(jnp.logical_and(right, z < NZ - 1))
        def _():
            send(buf.at[i], buf.at[i], ss.at[0, i], rs.at[i], at(z_=z + 1))

        @pl.when(jnp.logical_and(left, z > 0))
        def _():
            send(buf.at[i], buf.at[i], ss.at[1, i], rs.at[i], at(z_=z - 1))

    def line_step(buf, t, ss, rs):
        lo, hi = z - t, z + t

        @pl.when(lo >= 0)
        def _():
            arrived(buf.at[lo], rs.at[lo])
            line_out(buf, lo, ss, rs, True, False)

        @pl.when(hi < NZ)
        def _():
            arrived(buf.at[hi], rs.at[hi])
            line_out(buf, hi, ss, rs, False, True)

    def line_sent(buf, ss):
        for i in range(NZ):
            @pl.when(jnp.logical_and(i <= z, z < NZ - 1))
            def _():
                sent(buf.at[i], ss.at[0, i])

            @pl.when(jnp.logical_and(i >= z, z > 0))
            def _():
                sent(buf.at[i], ss.at[1, i])

    si[y, 0:1, :] = jnp.full((1, 128), slot[seg[0]], jnp.int32)
    si[y, 1:2, :] = jnp.full((1, 128), slot[seg[1]], jnp.int32)
    for k, p in enumerate(y_peers):
        send(si.at[y], si.at[y], si_s.at[k], si_r.at[y], at(y_=p))
    for k in range(NY):
        send(si.at[y], sin.at[y], sin_s.at[k], sin_r.at[y], at(s_=before, y_=k))
    uz[z] = up[...]
    line_out(uz, z, uz_s, uz_r, True, True)
    g_here = gf.at[x, pl.ds(pl.multiple_of(y * rows, rows), rows)]
    send(grad, g_here, shift_s.at[0], g_r.at[x, y], at(s_=before))
    send(wmat, wn.at[z], shift_s.at[1], w_r.at[z], at(s_=before))
    send(down, dns, shift_s.at[2], dns_r, at(s_=before))
    dz[z] = down[...]
    line_out(dz, z, dz_s, dz_r, True, True)

    def start_next():
        arrived(g_here, g_r.at[x, y])
        for k, p in enumerate(x_peers):
            send(g_here, g_here, g_sx.at[k, y], g_r.at[x, y], at(x_=p))
        for k, p in enumerate(y_peers):
            send(g_here, g_here, g_sy.at[k], g_r.at[x, y], at(y_=p))
        arrived(wn.at[z], w_r.at[z])
        line_out(wn, z, w_s, w_r, True, True)
        arrived(dns, dns_r)
        width = dn.shape[2]
        for k, p in enumerate(y_peers):
            cols = pl.ds(pl.multiple_of(p * width, width), width)
            mine = pl.ds(pl.multiple_of(y * rank, rank), rank)
            send(dns.at[:, cols], dn.at[z, mine], dna_s.at[k], dna_r.at[y], at(y_=p))
        own = pl.ds(pl.multiple_of(y * width, width), width)
        dn[z, pl.ds(pl.multiple_of(y * rank, rank), rank), :] = dns[:, own]

    @pl.when(first_core)
    def _():
        start_next()

    for p in y_peers:
        arrived(si.at[p], si_r.at[p])
    col = lax.broadcasted_iota(jnp.int32, (rank, 128), 1)
    row = lax.broadcasted_iota(jnp.int32, (rank, 128), 0)
    same = row == col % rank
    here = y * NZ + col // rank
    for p in range(NY):
        for k in range(2):
            ids = jnp.broadcast_to(si[p, k:k + 1, :], (rank, 128))
            hit = jnp.where(jnp.logical_and(ids == here, same), 1.0, 0.0)
            pm[pl.ds((p * 2 + k) * rank, rank), :] = hit.astype(BF16)

    for t in range(1, NZ):
        line_step(uz, t, uz_s, uz_r)
    usel[...] = nn_dot(pm[...], uz[...].reshape(NZ * rank, up.shape[1])).astype(BF16)
    mine64 = pl.ds(pl.multiple_of(y * 2 * rank, 2 * rank), 2 * rank)

    def rows_of(p):
        return pl.ds(pl.multiple_of(p * 2 * rank, 2 * rank), 2 * rank)

    for k, p in enumerate(y_peers):
        send(usel.at[rows_of(p)], ur.at[y], ur_s.at[k], ur_r.at[y], at(y_=p))
    ur[y] = usel[mine64, :]

    for t in range(1, NZ):
        line_step(dz, t, dz_s, dz_r)
    for j in range(4):
        c = slice(j * 512, (j + 1) * 512)
        dsel[:, c] = nn_dot(pm[...], dz[:, :, c].reshape(NZ * rank, 512)).astype(BF16)
    for k, p in enumerate(y_peers):
        send(dsel.at[rows_of(p)], dr.at[y], dr_s.at[k], dr_r.at[y], at(y_=p))
    dr[y] = dsel[mine64, :]

    for p in y_peers:
        arrived(ur.at[p], ur_r.at[p])
    picked = sum(ur[p].astype(F32) for p in range(NY)).astype(BF16)
    for k in range(2):
        lanes = slice(k * seg_rows, (k + 1) * seg_rows)
        rp[x, :, lanes] = nt_dot(picked[k * rank:(k + 1) * rank], grad[lanes, :])
    for k, p in enumerate(x_peers):
        send(rp.at[x], rp.at[x], rp_s.at[k], rp_r.at[x], at(x_=p))
    for p in x_peers:
        arrived(rp.at[p], rp_r.at[p])
    rt[...] = sum(rp[p] for p in range(NX)).astype(BF16)
    for k in range(NY):
        send(rt, rtn.at[y], rtn_s.at[k], rtn_r.at[y], at(s_=before, y_=k))
    for k in range(2):
        lanes = slice(k * seg_rows, (k + 1) * seg_rows)
        part = nn_dot(rt[:, lanes], act[lanes, :]) * norm
        pd[y, k * rank:(k + 1) * rank, :] = part.astype(BF16)
    for k, p in enumerate(y_peers):
        send(pd.at[y], pd.at[y], pd_s.at[k], pd_r.at[y], at(y_=p))

    for p in y_peers:
        arrived(dr.at[p], dr_r.at[p])
    for k in range(2):
        lanes = slice(k * seg_rows, (k + 1) * seg_rows)
        r32 = slice(k * rank, (k + 1) * rank)
        picked = sum(dr[p, r32, :].astype(F32) for p in range(NY)).astype(BF16)
        hp[x, :, lanes] = nt_dot(picked, act[lanes, :])
    for k, p in enumerate(x_peers):
        send(hp.at[x], hp.at[x], hp_s.at[k], hp_r.at[x], at(x_=p))

    for p in y_peers:
        arrived(pd.at[p], pd_r.at[p])
    for j in range(4):
        c = slice(j * 512, (j + 1) * 512)
        st[:, c] = tn_dot(pm[...], pd[:, :, c].reshape(NY * 2 * rank, 512)).astype(BF16)

    def rank_rows(p):
        return pl.ds(pl.multiple_of(p * rank, rank), rank)

    for k, p in enumerate(z_peers):
        send(st.at[rank_rows(p)], rsd.at[z], rsd_s.at[k], rsd_r.at[z], at(z_=p))
    rsd[z] = st[rank_rows(z), :]

    for p in x_peers:
        arrived(hp.at[p], hp_r.at[p])
    ht[...] = sum(hp[p] for p in range(NX)).astype(BF16)
    for k in range(2):
        lanes = slice(k * seg_rows, (k + 1) * seg_rows)
        part = nn_dot(ht[:, lanes], grad[lanes, :]) * norm
        pu[y, k * rank:(k + 1) * rank, :] = part.astype(BF16)
    for k, p in enumerate(y_peers):
        send(pu.at[y], pu.at[y], pu_s.at[k], pu_r.at[y], at(y_=p))

    @pl.when(jnp.logical_not(first_core))
    def _():
        start_next()

    for p in y_peers:
        arrived(pu.at[p], pu_r.at[p])
    su[...] = tn_dot(pm[...], pu[...].reshape(NY * 2 * rank, up.shape[1])).astype(BF16)
    for k, p in enumerate(z_peers):
        send(su.at[rank_rows(p)], rsu.at[z], rsu_s.at[k], rsu_r.at[z], at(z_=p))
    rsu[z] = su[rank_rows(z), :]

    def g_block(x_, y_):
        return gf.at[x_, pl.ds(pl.multiple_of(y_ * rows, rows), rows)]

    for p in y_peers:
        arrived(g_block(x, p), g_r.at[x, p])
        for k, q in enumerate(x_peers):
            send(g_block(x, p), g_block(x, p), g_sx.at[k, p], g_r.at[x, p], at(x_=q))
    for p in y_peers:
        arrived(dn.at[z, rank_rows(p)], dna_r.at[p])
    line_out(dn, z, dnz_s, dnz_r, True, True)

    spread = jnp.where(
        lax.broadcasted_iota(jnp.int32, (rank, rx.shape[1]), 0)
        == lax.broadcasted_iota(jnp.int32, (rank, rx.shape[1]), 1) % rank,
        ADAPTER_SCALE, 0.0,
    ).astype(BF16)
    cols = lax.broadcasted_iota(jnp.int32, (seg_rows, rx.shape[1]), 1)
    col_slot = (cols // rank) % NY * NZ + cols // (rank * NY)
    for p in range(NY):
        arrived(sin.at[p], sin_r.at[p])
        arrived(rtn.at[p], rtn_r.at[p])
        for k in range(2):
            wide = tn_dot(rtn[p, :, k * seg_rows:(k + 1) * seg_rows], spread)
            ids = jnp.broadcast_to(sin[p, k:k + 1, 0:1], wide.shape)
            rx[pl.ds(p * rows + k * seg_rows, seg_rows), :] = jnp.where(
                ids == col_slot, wide, 0.0
            ).astype(BF16)
    for t in range(1, NZ):
        line_step(dn, t, dnz_s, dnz_r)
    for q in x_peers:
        for p in range(NY):
            arrived(g_block(q, p), g_r.at[q, p])

    chunk = wmat.shape[0]

    def compute(i):
        lanes = pl.ds(pl.multiple_of(i * chunk, chunk), chunk)
        place = pl.ds(pl.multiple_of(y * (NZ * chunk) + i * chunk, chunk), chunk)
        for p in range(NY):
            r = slice(p * rows, (p + 1) * rows)
            total = nn_dot(rx[r, :], dn[:, :, lanes].reshape(rx.shape[1], chunk))
            for q in range(NX):
                total += nt_dot(gf[q, r, :], wn[i, :, q * rows:(q + 1) * rows])
            ot[i, r, :] = total.astype(BF16)
        for k, p in enumerate(y_peers):
            r = pl.ds(pl.multiple_of(p * rows, rows), rows)
            send(ot.at[i, r], out.at[:, place], o_s.at[k, i], o_r.at[y, i], at(y_=p))
        out[:, place] = ot[i, pl.ds(pl.multiple_of(y * rows, rows), rows), :]

    compute(z)

    @pl.loop(1, NZ)
    def _(t):
        lo, hi = z - t, z + t

        @pl.when(lo >= 0)
        def _():
            arrived(wn.at[lo], w_r.at[lo])
            line_out(wn, lo, w_s, w_r, True, False)

        @pl.when(hi < NZ)
        def _():
            arrived(wn.at[hi], w_r.at[hi])
            line_out(wn, hi, w_s, w_r, False, True)

        @pl.when(lo >= 0)
        def _():
            compute(lo)

        @pl.when(hi < NZ)
        def _():
            compute(hi)

    for p in z_peers:
        arrived(rsd.at[p], rsd_r.at[p])
    dgrad[...] = sum(rsd[p].astype(F32) for p in range(NZ)).astype(BF16)
    for p in z_peers:
        arrived(rsu.at[p], rsu_r.at[p])
    ugrad[...] = sum(rsu[p].astype(F32) for p in range(NZ)).astype(BF16)

    for p in y_peers:
        for i in range(NZ):
            place = pl.ds(pl.multiple_of((p * NZ + i) * chunk, chunk), chunk)
            arrived(out.at[:, place], o_r.at[p, i])
    sent(grad, shift_s.at[0])
    sent(wmat, shift_s.at[1])
    sent(down, shift_s.at[2])
    line_sent(uz, uz_s)
    line_sent(dz, dz_s)
    line_sent(dn, dnz_s)
    line_sent(wn, w_s)
    for k in range(NY):
        sent(si.at[0], sin_s.at[k])
        sent(rt, rtn_s.at[k])
    for k in range(3):
        sent(si.at[0], si_s.at[k])
        sent(g_here, g_sy.at[k])
        for p in range(NY):
            sent(g_here, g_sx.at[k, p])
        sent(dn.at[0, pl.ds(0, rank)], dna_s.at[k])
        sent(ur.at[0], ur_s.at[k])
        sent(dr.at[0], dr_s.at[k])
        sent(rp.at[0], rp_s.at[k])
        sent(hp.at[0], hp_s.at[k])
        sent(pd.at[0], pd_s.at[k])
        sent(pu.at[0], pu_s.at[k])
        sent(rsd.at[0], rsd_s.at[k])
        sent(rsu.at[0], rsu_s.at[k])
        for i in range(NZ):
            sent(ot.at[0, pl.ds(0, rows)], o_s.at[k, i])


def body(
    activations,
    value_gradient,
    value_matrix,
    adapter_down_weight,
    adapter_up_weight,
    segment_adapter,
    adapter_slot,
):
    rows, width = activations.shape[1:]
    values = value_gradient.shape[2]
    w_rows, v_width = value_matrix.shape[1:]
    rank = adapter_down_weight.shape[2]
    slots = adapter_slot.shape[0]
    piece = width // NY
    vmem = pl.BlockSpec(memory_space=pltpu.VMEM)
    smem = pl.BlockSpec(memory_space=pltpu.SMEM)
    dma = lambda *shape: pltpu.SemaphoreType.DMA(shape)
    scratch = [
        pltpu.VMEM((NZ, w_rows, v_width), BF16),
        pltpu.VMEM((NX, NY * rows, values), BF16),
        pltpu.VMEM((rank, width), BF16),
        pltpu.VMEM((NZ, NY * rank, piece), BF16),
        pltpu.VMEM((NY, 8, 128), jnp.int32),
        pltpu.VMEM((NY, 8, 128), jnp.int32),
        pltpu.VMEM((NZ, rank, values), BF16),
        pltpu.VMEM((NY * 2 * rank, values), BF16),
        pltpu.VMEM((NY, 2 * rank, values), BF16),
        pltpu.VMEM((NZ, rank, width), BF16),
        pltpu.VMEM((NY * 2 * rank, width), BF16),
        pltpu.VMEM((NY, 2 * rank, width), BF16),
        pltpu.VMEM((NY * 2 * rank, NZ * rank), BF16),
        pltpu.VMEM((NX, rank, rows), F32),
        pltpu.VMEM((8, 128), F32),
        pltpu.VMEM((rank, rows), BF16),
        pltpu.VMEM((NY, rank, rows), BF16),
        pltpu.VMEM((NY * rows, slots * rank), BF16),
        pltpu.VMEM((NX, rank, rows), F32),
        pltpu.VMEM((rank, rows), BF16),
        pltpu.VMEM((NY, 2 * rank, width), BF16),
        pltpu.VMEM((NZ * rank, width), BF16),
        pltpu.VMEM((NZ, rank, width), BF16),
        pltpu.VMEM((NY, 2 * rank, values), BF16),
        pltpu.VMEM((NZ * rank, values), BF16),
        pltpu.VMEM((NZ, rank, values), BF16),
        pltpu.VMEM((NZ, NY * rows, w_rows), BF16),
        dma(3), dma(NZ), dma(2, NZ), dma(NX, NY), dma(3), dma(3, NY),
        pltpu.SemaphoreType.DMA, dma(NY), dma(3), dma(NZ), dma(2, NZ),
        dma(NY), dma(3), dma(NY), dma(NY),
        dma(NZ), dma(2, NZ), dma(NY), dma(3),
        dma(NZ), dma(2, NZ), dma(NY), dma(3),
        dma(NX), dma(3), dma(NY), dma(NY),
        dma(NX), dma(3), dma(NY), dma(3), dma(NZ), dma(3),
        dma(NY), dma(3), dma(NZ), dma(3),
        dma(NY, NZ), dma(3, NZ),
    ]
    received, down_gradient, up_gradient = pl.pallas_call(
        kernel,
        out_shape=(
            jax.ShapeDtypeStruct((rows, width), BF16),
            jax.ShapeDtypeStruct((rank, width), BF16),
            jax.ShapeDtypeStruct((rank, values), BF16),
        ),
        in_specs=[vmem] * 5 + [smem] * 2,
        out_specs=(vmem, vmem, vmem),
        scratch_shapes=scratch,
        compiler_params=pltpu.CompilerParams(
            collective_id=0, has_side_effects=True, vmem_limit_bytes=48 << 20
        ),
        name="relay_backward",
    )(
        activations[0],
        value_gradient[0],
        value_matrix[0],
        adapter_down_weight[0, 0],
        adapter_up_weight[0, 0],
        segment_adapter[0],
        adapter_slot,
    )
    return received[None], down_gradient[None, None], up_gradient[None, None]


def solution(mesh):
    placed = (
        P("section", "dp", "mp"),
        P("section", "dp", "mp"),
        P("section", ("mp", "dp"), None),
        P("section", "dp", None, "mp"),
        P("section", "dp", None, "mp"),
        P("section", "dp"),
        P(),
    )
    return jax.shard_map(
        body,
        mesh=mesh,
        in_specs=placed,
        out_specs=(
            P("section", "dp", "mp"),
            P("section", "dp", None, "mp"),
            P("section", "dp", None, "mp"),
        ),
        check_vma=False,
    )
```

time: 432 us -> 118 us (0.27)
  waiting for transfers between devices: 319 us -> 0 us
  Pallas kernels: 0 us -> 109 us
  blocking collectives: 76.5 us -> 0 us
  between operations: 13.8 us -> 0.66 us
  matrix products: 9.72 us -> 0 us
  starting transfers between devices: 5.05 us -> 0 us
    reduce_scatter x2 -> x0, waiting for transfers between devices: 160 us -> none  [the longest x1 102 us: body(): lax.psum_scatter(slot_down.astype(jnp.bfloat16), 'dp', scatter_dimension=...]
    all_gather x2 -> x0, waiting for transfers between devices: 117 us -> none  [the longest x1 68 us: body(): lax.all_gather(value_matrix[0], 'dp', axis=0, tiled=True)]
    pallas_call x0 -> x1, Pallas kernels: none -> 109 us  [body(): pl.pallas_call(kernel, out_shape=(jax.ShapeDtypeStruct((rows, width), BF1...]
    all_gather x2 -> x0, blocking collectives: 60.5 us -> none  [the longest x1 46.9 us: body(): lax.all_gather(adapter_up_weight[0], 'dp', axis=0, tiled=True)]
    ppermute x1 -> x0, waiting for transfers between devices: 39.9 us -> none  [passed_along(): return lax.ppermute(block, axis, route)]
    psum x1 -> x0, blocking collectives: 16 us -> none  [body(): lax.psum(grad_part.astype(jnp.bfloat16), 'mp').astype(jnp.float32)]
    dot_general x10 -> x0, matrix products: 9.72 us -> none  [the longest x1 3.64 us: body(): jnp.einsum('tv,kv->tk', full_grad, lax.all_gather(value_matrix[0], 'dp',...]
    ppermute x1 -> x0, starting transfers between devices: 4.9 us -> none  [passed_along(): return lax.ppermute(block, axis, route)]
  transfers between devices with their start and end apart: 5 -> 0, of which waited for: 5 -> 0; matrix products, arithmetic and copies ran while one was open for 4% -> 0% of each run, Pallas kernels for 0% -> 0%
where the time goes in v1:
time: 118 us; the launch traced here: 117 us
  Pallas kernels  109 us (92%)
  local copies, waits for them, and re-layouts  7.59 us (6%)
    pallas_call x1, Pallas kernels, body(): pl.pallas_call(kernel, out_shape=(jax.ShapeDtypeStruct((rows, width), BF1...  109 us
    unnamed x17, local copies, waits for them, and re-layouts  7.59 us

profile of v1, /device:TPU:4, one launch (start us, length us, event | category | flops | bytes accessed | tf_op | source)
XLA Modules:
  0.0 117.4 jit_solution(17204890094699064513)
XLA Ops:
  0.6 0.0 copy-start.5
  0.6 0.0 copy-start.6
  0.7 0.6 copy-done.5
  1.3 0.0 copy-done.6
  1.3 0.0 copy-start
  1.3 1.2 %copy-done = bf16[1,256,2048]{2,1,0:T(8,128)(2,1)S(1)} copy-done((bf16[1,256,2048]{2,1,0:T(8,128)(2,1)S(1)}, bf16[1,256,2048]{2,1,0:T(8,128)(2,1)}, u32[]{:S(2)}) %copy-start) | copy-done | bytes 1048600
  2.5 0.0 copy-start.1
  2.5 0.9 copy-done.1
  3.5 0.0 copy-start.2
  3.5 0.9 copy-done.2
  4.4 0.0 copy-start.3
  4.4 0.9 copy-done.3
  5.3 0.0 copy-start.4
  5.3 0.7 copy-done.4
  6.0 109.2 %relay_backward.1 = (bf16[256,2048]{1,0:T(8,128)(2,1)S(1)}, bf16[32,2048]{1,0:T(8,128)(2,1)S(1)}, bf16[32,256]{1,0:T(8,128)(2,1)S(1)}) custom-call(bf16[256,2048]{1,0:T(8,128)(2,1)S(1)} %bitcast.9, bf16[256,256]{1,0:T(8,128)(2,1)S(1)} %bitcast.13, bf16[128,1024]{1,0:T(8,128)(2,1)S(1)} %bitcast.11, bf16[32,2048]{1,0:T(8,128)(2,1)S(1)} %bitcast.14, ...), custom_call_target="tpu_custom_call" | custom-call | tf_op jit(solution)/shard_map/relay_backward/pallas_call | solution.py:420
  115.2 1.0 copy.13
  116.2 0.7 copy.14
  116.8 0.6 copy.15
Async XLA Ops:
  0.6 0.7 copy-start.5
  0.6 0.7 copy-start.6
  1.3 1.2 %copy-start = (bf16[1,256,2048]{2,1,0:T(8,128)(2,1)S(1)}, bf16[1,256,2048]{2,1,0:T(8,128)(2,1)}, u32[]{:S(2)}) copy-start(bf16[1,256,2048]{2,1,0:T(8,128)(2,1)} %param.7) | copy-start | bytes 3145732
  2.5 0.9 copy-start.1
  3.5 0.9 copy-start.2
  4.4 0.9 copy-start.3
  5.3 0.7 copy-start.4

commit v2 on v0

v2 whole, which is shorter than its diff:
```python
import functools
import math

import jax
import jax.numpy as jnp
from jax import lax
from jax.experimental import pallas as pl
from jax.experimental.pallas import tpu as pltpu
from jax.sharding import PartitionSpec as P

ADAPTERS_PER_DP = 1
ADAPTER_SCALE = 2.0
MESH = pl.DeviceIdType.MESH
BF16 = jnp.bfloat16
F32 = jnp.float32

NY = 4
NZ = 4
NX = 4
NS = 8
NP = 2


def nt_dot(a, b):
    return lax.dot_general(a, b, (((1,), (1,)), ((), ())), preferred_element_type=F32)


def nn_dot(a, b):
    return lax.dot_general(a, b, (((1,), (0,)), ((), ())), preferred_element_type=F32)


def tn_dot(a, b):
    return lax.dot_general(a, b, (((0,), (0,)), ((), ())), preferred_element_type=F32)


def kernel(
    act_hbm, grad_hbm, wmat, down, up, seg, slot,
    out, dgrad, ugrad,
    act, grad, wn, gf, dns, dn, si, sin, uz, usel, ur, dz, dsel, dr,
    pm, rp, rt, rtn, rx, hp, ht, pd, st, rsd, pu, su, rsu, ot,
    local_s, shift_s, w_r, w_s, g_r, g_sy, g_sx, dns_r, dna_r, dna_s, dnz_r, dnz_s,
    si_r, si_s, sin_r, sin_s, uz_r, uz_s, ur_r, ur_s, dz_r, dz_s, dr_r, dr_s,
    rp_r, rp_s, rtn_r, rtn_s, hp_r, hp_s, pd_r, pd_s, rsd_r, rsd_s,
    pu_r, pu_s, rsu_r, rsu_s, o_r, o_s,
):
    s = lax.axis_index("section")
    d = lax.axis_index("dp")
    x = lax.axis_index("mp")
    y, z = d // NZ, d % NZ
    before, after = (s + NS - 1) % NS, (s + 1) % NS
    rows = act.shape[0]
    seg_rows = rows // 2
    rank = down.shape[0]
    piece = dn.shape[2]
    chunk = wmat.shape[0]
    wp = chunk // NP
    norm = ADAPTER_SCALE / math.sqrt(rows / ADAPTERS_PER_DP)

    def at(s_=s, y_=y, z_=z, x_=x):
        return {"section": s_, "dp": y_ * NZ + z_, "mp": x_}

    def copy(src, dst, ss, rs, device):
        return pltpu.make_async_remote_copy(
            src_ref=src, dst_ref=dst, send_sem=ss, recv_sem=rs,
            device_id=device, device_id_type=MESH,
        )

    def arrived(dst, rs):
        copy(dst, dst, rs, rs, at()).wait_recv()

    def sent(src, ss):
        copy(src, src, ss, ss, at()).wait_send()

    def block(i, n):
        return pl.ds(i * n, n) if isinstance(i, int) else pl.ds(pl.multiple_of(i * n, n), n)

    y_peers = [(y + k) % NY for k in (1, 3, 2)]
    x_peers = [(x + k) % NX for k in (1, 3, 2)]
    z_peers = [(z + k) % NZ for k in (1, 2, 3)]
    segments = [slice(k * seg_rows, (k + 1) * seg_rows) for k in range(2)]
    ranks = [slice(k * rank, (k + 1) * rank) for k in range(2)]
    wide = 2 * rank
    columns = [slice(j, j + 512) for j in range(0, act.shape[1], 512)]
    who = [None]
    started = []

    def send(like, src, dst, ss, rs, device, when=None):
        started.append((who[0], when, like, ss))

        def start():
            copy(src, dst, ss[0].at[ss[1:]], rs, device).start()

        if when is None:
            start()
        else:
            pl.when(when())(start)

    def on(core, *steps):
        who[0] = core

        def run():
            for step in steps:
                step()

        if core is None:
            run()
        else:
            pl.when(s % 2 == core)(run)
        who[0] = None

    loads = [
        pltpu.make_async_copy(src, dst, local_s.at[k])
        for k, (src, dst) in enumerate(
            [(up, uz.at[z]), (grad_hbm, grad), (down, dz.at[z]), (act_hbm, act)]
        )
    ]
    for load in loads:
        load.start()

    bar = pltpu.get_barrier_semaphore()
    peers = (
        [at(y_=p) for p in y_peers] + [at(x_=p) for p in x_peers] + [at(z_=p) for p in z_peers]
        + [at(s_=before, y_=k) for k in range(NY)] + [at(s_=after, y_=k) for k in range(NY)]
    )
    for p in peers:
        pl.semaphore_signal(bar, inc=1, device_id=p, device_id_type=MESH)
    si[y, 0:1, :] = jnp.full((1, 128), slot[seg[0]], jnp.int32)
    si[y, 1:2, :] = jnp.full((1, 128), slot[seg[1]], jnp.int32)
    pl.semaphore_wait(bar, len(peers))

    def g_block(x_, y_):
        return gf.at[x_, block(y_, rows)]

    def w_piece(i, p):
        return wn.at[i, p * wp:(p + 1) * wp]

    def slots_out():
        for k, p in enumerate(y_peers):
            send(lambda: si.at[0], si.at[y], si.at[y], (si_s, k), si_r.at[y], at(y_=p))

    def up_out():
        for k, p in enumerate(z_peers):
            send(up, up, uz.at[z], (uz_s, k), uz_r.at[z], at(z_=p))

    def down_out():
        for k, p in enumerate(z_peers):
            send(down, down, dz.at[z], (dz_s, k), dz_r.at[z], at(z_=p))

    def slots_next_out():
        for k in range(NY):
            send(lambda: si.at[0], si.at[y], sin.at[y], (sin_s, k), sin_r.at[y], at(s_=before, y_=k))

    def w_shift():
        for p in range(NP):
            send(lambda p=p: w_piece(0, p), wmat.at[p * wp:(p + 1) * wp], w_piece(z, p), (shift_s, p), w_r.at[z, p], at(s_=before))

    def g_shift():
        send(grad, grad_hbm, g_block(x, y), (shift_s, NP), g_r.at[x, y], at(s_=before))

    def down_shift():
        send(dns, down, dns, (shift_s, NP + 1), dns_r, at(s_=before))

    def g_start_y():
        arrived(g_block(x, y), g_r.at[x, y])
        for k, p in enumerate(y_peers):
            send(grad, g_block(x, y), g_block(x, y), (g_sy, k), g_r.at[x, y], at(y_=p))

    def g_start_x():
        for k, p in enumerate(x_peers):
            send(grad, g_block(x, y), g_block(x, y), (g_sx, k, 0), g_r.at[x, y], at(x_=p))

    def g_relay():
        for j, p in enumerate(y_peers):
            arrived(g_block(x, p), g_r.at[x, p])
            for k, q in enumerate(x_peers):
                send(grad, g_block(x, p), g_block(x, p), (g_sx, k, 1 + j), g_r.at[x, p], at(x_=q))

    def w_out(t, p, way):
        i, z_to = (z - t, z + 1) if way == 0 else (z + t, z - 1)

        def when():
            if way == 0:
                return jnp.logical_and(z < NZ - 1, z >= t)
            return jnp.logical_and(z > 0, z < NZ - t)

        send(lambda p=p: w_piece(0, p), w_piece(i, p), w_piece(i, p), (w_s, way, t, p), w_r.at[i, p], at(z_=z_to), when)

    def w_start():
        for p in range(NP):
            arrived(w_piece(z, p), w_r.at[z, p])
            w_out(0, p, 1)
            w_out(0, p, 0)

    def w_step(t):
        lo, hi = z - t, z + t
        for p in range(NP):
            pl.when(hi < NZ)(functools.partial(arrived, w_piece(hi, p), w_r.at[hi, p]))
            w_out(t, p, 1)
            pl.when(lo >= 0)(functools.partial(arrived, w_piece(lo, p), w_r.at[lo, p]))
            w_out(t, p, 0)

    def picks():
        for p in y_peers:
            arrived(si.at[p], si_r.at[p])
        col = lax.broadcasted_iota(jnp.int32, (rank, 128), 1)
        row = lax.broadcasted_iota(jnp.int32, (rank, 128), 0)
        same = row == col % rank
        here = y * NZ + col // rank
        for p in range(NY):
            for k in range(2):
                ids = jnp.broadcast_to(si[p, k:k + 1, :], (rank, 128))
                hit = jnp.where(jnp.logical_and(ids == here, same), 1.0, 0.0)
                pm[pl.ds((p * 2 + k) * rank, rank), :] = hit.astype(BF16)

    def up_pick():
        loads[0].wait()
        for p in z_peers:
            arrived(uz.at[p], uz_r.at[p])
        usel[...] = nn_dot(pm[...], uz[...].reshape(NZ * rank, up.shape[1])).astype(BF16)
        for k, p in enumerate(y_peers):
            send(lambda: ur.at[0], usel.at[block(p, wide)], ur.at[y], (ur_s, k), ur_r.at[y], at(y_=p))
        ur[y] = usel[block(y, wide), :]

    def rank_part():
        loads[1].wait()
        for p in y_peers:
            arrived(ur.at[p], ur_r.at[p])
        picked = sum(ur[p].astype(F32) for p in range(NY)).astype(BF16)
        for r, lanes in zip(ranks, segments):
            rp[x, :, lanes] = nt_dot(picked[r], grad[lanes, :])
        for k, p in enumerate(x_peers):
            send(lambda: rp.at[0], rp.at[x], rp.at[x], (rp_s, k), rp_r.at[x], at(x_=p))

    def rank_sum():
        for p in x_peers:
            arrived(rp.at[p], rp_r.at[p])
        rt[...] = sum(rp[p] for p in range(NX)).astype(BF16)
        for k in range(NY):
            send(rt, rt, rtn.at[y], (rtn_s, k), rtn_r.at[y], at(s_=before, y_=k))

    def down_part():
        loads[3].wait()
        for r, lanes in zip(ranks, segments):
            pd[y, r, :] = (nn_dot(rt[:, lanes], act[lanes, :]) * norm).astype(BF16)
        for k, p in enumerate(y_peers):
            send(lambda: pd.at[0], pd.at[y], pd.at[y], (pd_s, k), pd_r.at[y], at(y_=p))

    def down_sum():
        for p in y_peers:
            arrived(pd.at[p], pd_r.at[p])
        for c in columns:
            st[:, c] = tn_dot(pm[...], pd[:, :, c].reshape(NY * wide, 512)).astype(BF16)
        for k, p in enumerate(z_peers):
            send(lambda: rsd.at[0], st.at[block(p, rank)], rsd.at[z], (rsd_s, k), rsd_r.at[z], at(z_=p))
        rsd[z] = st[block(z, rank), :]

    def down_end():
        for p in z_peers:
            arrived(rsd.at[p], rsd_r.at[p])
        dgrad[...] = sum(rsd[p].astype(F32) for p in range(NZ)).astype(BF16)

    def down_wait():
        loads[2].wait()
        for p in z_peers:
            arrived(dz.at[p], dz_r.at[p])

    def down_next():
        for k in range(NY):
            send(lambda: dn.at[:, block(0, rank)], dz.at[:, :, block(k, piece)], dn.at[:, block(y, rank)],
                 (dna_s, k), dna_r.at[y], at(s_=before, y_=k))

    def down_pick():
        for c in columns:
            dsel[:, c] = nn_dot(pm[...], dz[:, :, c].reshape(NZ * rank, 512)).astype(BF16)
        for k, p in enumerate(y_peers):
            send(lambda: dr.at[0], dsel.at[block(p, wide)], dr.at[y], (dr_s, k), dr_r.at[y], at(y_=p))
        dr[y] = dsel[block(y, wide), :]

    def hidden_part():
        for p in y_peers:
            arrived(dr.at[p], dr_r.at[p])
        for r, lanes in zip(ranks, segments):
            picked = sum(dr[p, r, :].astype(F32) for p in range(NY)).astype(BF16)
            hp[x, :, lanes] = nt_dot(picked, act[lanes, :])
        for k, p in enumerate(x_peers):
            send(lambda: hp.at[0], hp.at[x], hp.at[x], (hp_s, k), hp_r.at[x], at(x_=p))

    def up_part():
        for p in x_peers:
            arrived(hp.at[p], hp_r.at[p])
        ht[...] = sum(hp[p] for p in range(NX)).astype(BF16)
        for r, lanes in zip(ranks, segments):
            pu[y, r, :] = (nn_dot(ht[:, lanes], grad[lanes, :]) * norm).astype(BF16)
        for k, p in enumerate(y_peers):
            send(lambda: pu.at[0], pu.at[y], pu.at[y], (pu_s, k), pu_r.at[y], at(y_=p))

    def up_sum():
        for p in y_peers:
            arrived(pu.at[p], pu_r.at[p])
        su[...] = tn_dot(pm[...], pu[...].reshape(NY * wide, up.shape[1])).astype(BF16)
        for k, p in enumerate(z_peers):
            send(lambda: rsu.at[0], su.at[block(p, rank)], rsu.at[z], (rsu_s, k), rsu_r.at[z], at(z_=p))
        rsu[z] = su[block(z, rank), :]

    def up_end():
        for p in z_peers:
            arrived(rsu.at[p], rsu_r.at[p])
        ugrad[...] = sum(rsu[p].astype(F32) for p in range(NZ)).astype(BF16)

    def dn_start():
        arrived(dns, dns_r)
        for k, p in enumerate(y_peers):
            send(lambda: dn.at[0, block(0, rank)], dns.at[:, block(p, piece)], dn.at[z, block(y, rank)],
                 (dna_s, NY + k), dna_r.at[y], at(y_=p))
        dn[z, block(y, rank), :] = dns[:, block(y, piece)]

    def dn_relay():
        for p in y_peers:
            arrived(dn.at[z, block(p, rank)], dna_r.at[p])
        for k, p in enumerate(z_peers):
            send(lambda: dn.at[0], dn.at[z], dn.at[z], (dnz_s, k), dnz_r.at[z], at(z_=p))

    def dn_wait0():
        for p in range(NY):
            arrived(dn.at[:, block(p, rank)], dna_r.at[p])

    def dn_wait1():
        for p in z_peers:
            arrived(dn.at[p], dnz_r.at[p])

    slots_wide = rx.shape[1]

    def rank_spread():
        spread = jnp.where(
            lax.broadcasted_iota(jnp.int32, (rank, slots_wide), 0)
            == lax.broadcasted_iota(jnp.int32, (rank, slots_wide), 1) % rank,
            ADAPTER_SCALE, 0.0,
        ).astype(BF16)
        cols = lax.broadcasted_iota(jnp.int32, (seg_rows, slots_wide), 1)
        col_slot = (cols // rank) % NY * NZ + cols // (rank * NY)
        for p in range(NY):
            arrived(sin.at[p], sin_r.at[p])
            arrived(rtn.at[p], rtn_r.at[p])
            for k, lanes in enumerate(segments):
                spread_out = tn_dot(rtn[p, :, lanes], spread)
                ids = jnp.broadcast_to(sin[p, k:k + 1, 0:1], spread_out.shape)
                rx[pl.ds(p * rows + k * seg_rows, seg_rows), :] = jnp.where(
                    ids == col_slot, spread_out, 0.0
                ).astype(BF16)

    def g_wait():
        for q in x_peers:
            for p in range(NY):
                arrived(g_block(q, p), g_r.at[q, p])

    def product(i):
        place = block(y * NZ + i, chunk)
        for p in range(NY):
            r = slice(p * rows, (p + 1) * rows)
            total = nn_dot(rx[r, :], dn[:, :, block(i, chunk)].reshape(slots_wide, chunk))
            for q in range(NX):
                total += nt_dot(gf[q, r, :], wn[i, :, q * rows:(q + 1) * rows])
            ot[i, r, :] = total.astype(BF16)
        for k, p in enumerate(y_peers):
            copy(ot.at[i, block(p, rows)], out.at[:, place], o_s.at[k, i], o_r.at[y, i], at(y_=p)).start()
        out[:, place] = ot[i, block(y, rows), :]

    def products():
        @pl.loop(0, NZ)
        def _(t):
            for side, i in enumerate((z - t, z + t)):
                @pl.when(i >= 0 if side == 0 else jnp.logical_and(i < NZ, t > 0))
                def _():
                    @pl.when(t == NZ - 1)
                    def _():
                        for p in range(NP):
                            arrived(w_piece(i, p), w_r.at[i, p])
                    product(i)

        for i in range(NZ):
            for k in range(3):
                started.append((who[0], None, lambda: ot.at[0, block(0, rows)], (o_s, k, i)))

    def out_end():
        for p in y_peers:
            for i in range(NZ):
                arrived(out.at[:, block(p * NZ + i, chunk)], o_r.at[p, i])

    def w_step1():
        w_step(1)

    def w_step2():
        w_step(2)

    on(None, slots_out, up_out, w_shift, g_shift)
    on(0, down_shift)
    on(None, down_out, slots_next_out)
    on(0, w_start, g_start_y, g_start_x)
    on(None, picks, up_pick)
    on(0, g_relay)
    on(None, rank_part, rank_sum, down_part)
    on(0, w_step1)
    on(None, rank_spread)
    on(1, w_start, g_start_y, g_start_x, dn_start)
    on(None, down_wait)
    on(1, down_next)
    on(None, down_pick)
    on(0, w_step2)
    on(1, w_step1, g_relay, dn_relay)
    on(None, down_sum)
    on(1, w_step2)
    on(None, hidden_part)
    on(0, dn_wait0, g_wait, products)
    on(None, up_part)
    on(1, dn_wait1, g_wait, products)
    on(None, up_sum, down_end, up_end, out_end)

    for core in (None, 0, 1):
        group = [e[1:] for e in started if e[0] == core]

        def finish():
            for when, like, ss in group:
                def wait():
                    sent(like() if callable(like) else like, ss[0].at[ss[1:]])

                if when is None:
                    wait()
                else:
                    pl.when(when())(wait)

        on(core, finish)


def body(
    activations,
    value_gradient,
    value_matrix,
    adapter_down_weight,
    adapter_up_weight,
    segment_adapter,
    adapter_slot,
):
    rows, width = activations.shape[1:]
    values = value_gradient.shape[2]
    w_rows, v_width = value_matrix.shape[1:]
    rank = adapter_down_weight.shape[2]
    slots = adapter_slot.shape[0]
    piece = width // NY
    vmem = pl.BlockSpec(memory_space=pltpu.VMEM)
    hbm = pl.BlockSpec(memory_space=pltpu.HBM)
    smem = pl.BlockSpec(memory_space=pltpu.SMEM)
    dma = lambda *shape: pltpu.SemaphoreType.DMA(shape)
    scratch = [
        pltpu.VMEM((rows, width), BF16),
        pltpu.VMEM((rows, values), BF16),
        pltpu.VMEM((NZ, w_rows, v_width), BF16),
        pltpu.VMEM((NX, NY * rows, values), BF16),
        pltpu.VMEM((rank, width), BF16),
        pltpu.VMEM((NZ, NY * rank, piece), BF16),
        pltpu.VMEM((NY, 8, 128), jnp.int32),
        pltpu.VMEM((NY, 8, 128), jnp.int32),
        pltpu.VMEM((NZ, rank, values), BF16),
        pltpu.VMEM((NY * 2 * rank, values), BF16),
        pltpu.VMEM((NY, 2 * rank, values), BF16),
        pltpu.VMEM((NZ, rank, width), BF16),
        pltpu.VMEM((NY * 2 * rank, width), BF16),
        pltpu.VMEM((NY, 2 * rank, width), BF16),
        pltpu.VMEM((NY * 2 * rank, NZ * rank), BF16),
        pltpu.VMEM((NX, rank, rows), F32),
        pltpu.VMEM((rank, rows), BF16),
        pltpu.VMEM((NY, rank, rows), BF16),
        pltpu.VMEM((NY * rows, slots * rank), BF16),
        pltpu.VMEM((NX, rank, rows), F32),
        pltpu.VMEM((rank, rows), BF16),
        pltpu.VMEM((NY, 2 * rank, width), BF16),
        pltpu.VMEM((NZ * rank, width), BF16),
        pltpu.VMEM((NZ, rank, width), BF16),
        pltpu.VMEM((NY, 2 * rank, values), BF16),
        pltpu.VMEM((NZ * rank, values), BF16),
        pltpu.VMEM((NZ, rank, values), BF16),
        pltpu.VMEM((NZ, NY * rows, w_rows), BF16),
        dma(4), dma(NP + 2), dma(NZ, NP), dma(2, NZ, NP),
        dma(NX, NY), dma(3), dma(3, NY),
        pltpu.SemaphoreType.DMA, dma(NY), dma(NY + 3), dma(NZ), dma(3),
        dma(NY), dma(3), dma(NY), dma(NY),
        dma(NZ), dma(3), dma(NY), dma(3),
        dma(NZ), dma(3), dma(NY), dma(3),
        dma(NX), dma(3), dma(NY), dma(NY),
        dma(NX), dma(3), dma(NY), dma(3), dma(NZ), dma(3),
        dma(NY), dma(3), dma(NZ), dma(3),
        dma(NY, NZ), dma(3, NZ),
    ]
    received, down_gradient, up_gradient = pl.pallas_call(
        kernel,
        out_shape=(
            jax.ShapeDtypeStruct((rows, width), BF16),
            jax.ShapeDtypeStruct((rank, width), BF16),
            jax.ShapeDtypeStruct((rank, values), BF16),
        ),
        in_specs=[hbm] * 5 + [smem] * 2,
        out_specs=(vmem, vmem, vmem),
        scratch_shapes=scratch,
        compiler_params=pltpu.CompilerParams(
            collective_id=0, has_side_effects=True, vmem_limit_bytes=63 << 20
        ),
        name="relay_backward",
    )(
        activations[0],
        value_gradient[0],
        value_matrix[0],
        adapter_down_weight[0, 0],
        adapter_up_weight[0, 0],
        segment_adapter[0],
        adapter_slot,
    )
    return received[None], down_gradient[None, None], up_gradient[None, None]


def solution(mesh):
    placed = (
        P("section", "dp", "mp"),
        P("section", "dp", "mp"),
        P("section", ("mp", "dp"), None),
        P("section", "dp", None, "mp"),
        P("section", "dp", None, "mp"),
        P("section", "dp"),
        P(),
    )
    return jax.shard_map(
        body,
        mesh=mesh,
        in_specs=placed,
        out_specs=(
            P("section", "dp", "mp"),
            P("section", "dp", None, "mp"),
            P("section", "dp", None, "mp"),
        ),
        check_vma=False,
    )
```

time: 432 us -> 99.7 us (0.23)
  the two profiles are of different devices: /device:TPU:4 before, /device:TPU:1 now
where the time goes in v2:
time: 99.7 us; the launch traced here: 99.5 us
  Pallas kernels  95.1 us (95%)
  local copies, waits for them, and re-layouts  3.67 us (4%)
    pallas_call x1, Pallas kernels, body(): pl.pallas_call(kernel, out_shape=(jax.ShapeDtypeStruct((rows, width), BF1...  95.1 us
    unnamed x7, local copies, waits for them, and re-layouts  3.67 us

profile of v2, /device:TPU:1, one launch (start us, length us, event | category | flops | bytes accessed | tf_op | source)
XLA Modules:
  0.0 99.5 jit_solution(5676482653849258378)
XLA Ops:
  0.6 95.1 %relay_backward.1 = (bf16[256,2048]{1,0:T(8,128)(2,1)}, bf16[32,2048]{1,0:T(8,128)(2,1)}, bf16[32,256]{1,0:T(8,128)(2,1)}) custom-call(bf16[256,2048]{1,0:T(8,128)(2,1)} %bitcast.9, bf16[256,256]{1,0:T(8,128)(2,1)} %bitcast.13, bf16[128,1024]{1,0:T(8,128)(2,1)} %bitcast.11, bf16[32,2048]{1,0:T(8,128)(2,1)} %bitcast.14, bf16[32,256]{1,0:T(8,128)(2,1)} %bitcast.15, ...), custom_call_target="tpu_custom_call" | custom-call | tf_op jit(solution)/shard_map/relay_backward/pallas_call | solution.py:493
  95.8 0.0 copy-start
  95.8 2.3 %copy.13 = bf16[1,256,2048]{2,1,0:T(8,128)(2,1)} copy(bf16[1,256,2048]{2,1,0:T(8,128)(2,1)} %bitcast.10) | data formatting | bytes 2097152
  98.1 0.0 copy-done
  98.1 0.0 copy-start.1
  98.1 0.7 copy.14
  98.8 0.1 copy-done.1
  98.9 0.6 copy.15
Async XLA Ops:
  95.8 2.4 %copy-start = (bf16[32,2048]{1,0:T(8,128)(2,1)S(1)}, bf16[32,2048]{1,0:T(8,128)(2,1)}, u32[]{:S(2)}) copy-start(bf16[32,2048]{1,0:T(8,128)(2,1)} %get-tuple-element.7) | copy-start | bytes 393220
  98.1 0.7 copy-start.1

commit v3 on v2

--- a/solution.py
+++ b/solution.py
@@ -36,9 +36,9 @@
 def kernel(
     act_hbm, grad_hbm, wmat, down, up, seg, slot,
     out, dgrad, ugrad,
-    act, grad, wn, gf, dns, dn, si, sin, uz, usel, ur, dz, dsel, dr,
+    act, grad, wn, gf, dns, far, dn, si, sin, uz, usel, ur, dz, dsel, dr,
     pm, rp, rt, rtn, rx, hp, ht, pd, st, rsd, pu, su, rsu, ot,
-    local_s, shift_s, w_r, w_s, g_r, g_sy, g_sx, dns_r, dna_r, dna_s, dnz_r, dnz_s,
+    local_s, shift_s, w_r, w_s, g_r, g_sy, g_sx, far_r, far_s, dns_r, dna_r, dna_s, dnz_r, dnz_s,
     si_r, si_s, sin_r, sin_s, uz_r, uz_s, ur_r, ur_s, dz_r, dz_s, dr_r, dr_s,
     rp_r, rp_s, rtn_r, rtn_s, hp_r, hp_s, pd_r, pd_s, rsd_r, rsd_s,
     pu_r, pu_s, rsu_r, rsu_s, o_r, o_s,
@@ -121,6 +121,7 @@
     peers = (
         [at(y_=p) for p in y_peers] + [at(x_=p) for p in x_peers] + [at(z_=p) for p in z_peers]
         + [at(s_=before, y_=k) for k in range(NY)] + [at(s_=after, y_=k) for k in range(NY)]
+        + [at(s_=(s + 2) % NS), at(s_=(s + 6) % NS), at(s_=(s + 3 + 2 * (s % 2)) % NS)]
     )
     for p in peers:
         pl.semaphore_signal(bar, inc=1, device_id=p, device_id_type=MESH)
@@ -157,8 +158,16 @@
     def g_shift():
         send(grad, grad_hbm, g_block(x, y), (shift_s, NP), g_r.at[x, y], at(s_=before))
 
-    def down_shift():
-        send(dns, down, dns, (shift_s, NP + 1), dns_r, at(s_=before))
+    def far0():
+        send(down, down, far.at[0], (far_s, 0), far_r.at[0], at(s_=(s + 2) % NS))
+
+    def far1():
+        arrived(far.at[0], far_r.at[0])
+        send(dns, far.at[0], far.at[1], (far_s, 1), far_r.at[1], at(s_=(s + 2) % NS))
+
+    def far2():
+        arrived(far.at[1], far_r.at[1])
+        send(dns, far.at[1], dns, (far_s, 2), dns_r, at(s_=(s + 3) % NS))
 
     def g_start_y():
         arrived(g_block(x, y), g_r.at[x, y])
@@ -245,19 +254,55 @@
         for k, p in enumerate(y_peers):
             send(lambda: pd.at[0], pd.at[y], pd.at[y], (pd_s, k), pd_r.at[y], at(y_=p))
 
+    def down_way(way, q, when):
+        z_to = z - 1 if way == 0 else z + 1
+        send(lambda: rsd.at[0, 0], rsd.at[way, q], rsd.at[way, q], (rsd_s, way, q), rsd_r.at[way, q], at(z_=z_to), when)
+
     def down_sum():
         for p in y_peers:
             arrived(pd.at[p], pd_r.at[p])
         for c in columns:
-            st[:, c] = tn_dot(pm[...], pd[:, :, c].reshape(NY * wide, 512)).astype(BF16)
-        for k, p in enumerate(z_peers):
-            send(lambda: rsd.at[0], st.at[block(p, rank)], rsd.at[z], (rsd_s, k), rsd_r.at[z], at(z_=p))
-        rsd[z] = st[block(z, rank), :]
+            st[:, :, c] = tn_dot(pm[...], pd[:, :, c].reshape(NY * wide, 512)).astype(BF16).reshape(NZ, rank, 512)
+
+        @pl.when(z == NZ - 1)
+        def _():
+            for q in range(NZ - 1):
+                rsd[0, q] = st[q]
+
+        @pl.when(z == 0)
+        def _():
+            for q in range(1, NZ):
+                rsd[1, q] = st[q]
+
+        for q in range(NZ - 1):
+            down_way(0, q, lambda: z == NZ - 1)
+        for q in range(NZ - 1, 0, -1):
+            down_way(1, q, lambda: z == 0)
+
+    def down_hop(way, q, here):
+        @pl.when(z == here)
+        def _():
+            arrived(rsd.at[way, q], rsd_r.at[way, q])
+            rsd[way, q] = (rsd[way, q].astype(F32) + st[q].astype(F32)).astype(BF16)
+
+        down_way(way, q, lambda: z == here)
+
+    def down_hop1():
+        for k in range(2):
+            down_hop(0, k, 2)
+            down_hop(1, 3 - k, 1)
+
+    def down_hop2():
+        down_hop(0, 0, 1)
+        down_hop(1, 3, 2)
 
     def down_end():
-        for p in z_peers:
-            arrived(rsd.at[p], rsd_r.at[p])
-        dgrad[...] = sum(rsd[p].astype(F32) for p in range(NZ)).astype(BF16)
+        pl.when(z < NZ - 1)(lambda: arrived(rsd.at[0, z], rsd_r.at[0, z]))
+        pl.when(z > 0)(lambda: arrived(rsd.at[1, z], rsd_r.at[1, z]))
+        total = st[z].astype(F32)
+        total += jnp.where(z < NZ - 1, rsd[0, z].astype(F32), 0.0)
+        total += jnp.where(z > 0, rsd[1, z].astype(F32), 0.0)
+        dgrad[...] = total.astype(BF16)
 
     def down_wait():
         loads[2].wait()
@@ -355,28 +400,39 @@
 
     def product(i):
         place = block(y * NZ + i, chunk)
-        for p in range(NY):
-            r = slice(p * rows, (p + 1) * rows)
+
+        @pl.loop(0, NY)
+        def _(p):
+            r = block(p, rows)
             total = nn_dot(rx[r, :], dn[:, :, block(i, chunk)].reshape(slots_wide, chunk))
             for q in range(NX):
                 total += nt_dot(gf[q, r, :], wn[i, :, q * rows:(q + 1) * rows])
             ot[i, r, :] = total.astype(BF16)
+
         for k, p in enumerate(y_peers):
             copy(ot.at[i, block(p, rows)], out.at[:, place], o_s.at[k, i], o_r.at[y, i], at(y_=p)).start()
         out[:, place] = ot[i, block(y, rows), :]
 
-    def products():
-        @pl.loop(0, NZ)
-        def _(t):
-            for side, i in enumerate((z - t, z + t)):
-                @pl.when(i >= 0 if side == 0 else jnp.logical_and(i < NZ, t > 0))
-                def _():
-                    @pl.when(t == NZ - 1)
-                    def _():
-                        for p in range(NP):
-                            arrived(w_piece(i, p), w_r.at[i, p])
-                    product(i)
-
+    def product_step(t):
+        for side, i in enumerate((z - t, z + t) if t else (z,)):
+            @pl.when(i >= 0 if side == 0 else i < NZ)
+            def _():
+                if t == NZ - 1:
+                    for p in range(NP):
+                        arrived(w_piece(i, p), w_r.at[i, p])
+                product(i)
+
+    def product0():
+        product_step(0)
+
+    def product1():
+        product_step(1)
+
+    def product2():
+        product_step(2)
+
+    def product3():
+        product_step(3)
         for i in range(NZ):
             for k in range(3):
                 started.append((who[0], None, lambda: ot.at[0, block(0, rows)], (o_s, k, i)))
@@ -392,28 +448,42 @@
     def w_step2():
         w_step(2)
 
-    on(None, slots_out, up_out, w_shift, g_shift)
-    on(0, down_shift)
-    on(None, down_out, slots_next_out)
-    on(0, w_start, g_start_y, g_start_x)
-    on(None, picks, up_pick)
-    on(0, g_relay)
+    on(1, slots_out, up_out, g_shift)
+    on(0, slots_out)
+    on(1, slots_next_out)
+    on(0, g_shift)
+    on(1, w_shift)
+    on(0, far0, up_out, far1, g_start_y)
+    on(None, picks)
+    on(0, w_start, slots_next_out)
+    on(1, down_out)
+    on(None, up_pick)
+    on(0, down_out)
     on(None, rank_part, rank_sum, down_part)
+    on(0, g_start_x, w_shift)
+    on(1, g_start_y)
+    on(0, down_wait, g_relay)
+    on(1, down_wait)
+    on(None, down_pick)
     on(0, w_step1)
-    on(None, rank_spread)
-    on(1, w_start, g_start_y, g_start_x, dn_start)
-    on(None, down_wait)
-    on(1, down_next)
-    on(None, down_pick)
-    on(0, w_step2)
-    on(1, w_step1, g_relay, dn_relay)
+    on(1, g_start_x)
+    on(0, far2)
+    on(1, g_relay, dn_start, w_start, down_next)
     on(None, down_sum)
-    on(1, w_step2)
+    on(1, rank_spread)
+    on(0, w_step2, rank_spread, g_wait, dn_wait0)
+    on(1, w_step1)
+    on(0, product0, product1)
     on(None, hidden_part)
-    on(0, dn_wait0, g_wait, products)
-    on(None, up_part)
-    on(1, dn_wait1, g_wait, products)
-    on(None, up_sum, down_end, up_end, out_end)
+    on(1, dn_relay)
+    on(0, product2)
+    on(1, w_step2, g_wait, dn_wait1)
+    on(None, down_hop1, up_part)
+    on(1, product0, product1)
+    on(0, product3)
+    on(None, down_hop2)
+    on(1, product2, product3)
+    on(None, up_sum, up_end, down_end, out_end)
 
     for core in (None, 0, 1):
         group = [e[1:] for e in started if e[0] == core]
@@ -456,6 +526,7 @@
         pltpu.VMEM((NZ, w_rows, v_width), BF16),
         pltpu.VMEM((NX, NY * rows, values), BF16),
         pltpu.VMEM((rank, width), BF16),
+        pltpu.VMEM((2, rank, width), BF16),
         pltpu.VMEM((NZ, NY * rank, piece), BF16),
         pltpu.VMEM((NY, 8, 128), jnp.int32),
         pltpu.VMEM((NY, 8, 128), jnp.int32),
@@ -473,22 +544,28 @@
         pltpu.VMEM((NX, rank, rows), F32),
         pltpu.VMEM((rank, rows), BF16),
         pltpu.VMEM((NY, 2 * rank, width), BF16),
-        pltpu.VMEM((NZ * rank, width), BF16),
         pltpu.VMEM((NZ, rank, width), BF16),
+        pltpu.VMEM((2, NZ, rank, width), BF16),
         pltpu.VMEM((NY, 2 * rank, values), BF16),
         pltpu.VMEM((NZ * rank, values), BF16),
         pltpu.VMEM((NZ, rank, values), BF16),
         pltpu.VMEM((NZ, NY * rows, w_rows), BF16),
-        dma(4), dma(NP + 2), dma(NZ, NP), dma(2, NZ, NP),
-        dma(NX, NY), dma(3), dma(3, NY),
+        dma(4), dma(NP + 1), dma(NZ, NP), dma(2, NZ, NP),
+        dma(NX, NY), dma(3), dma(3, NY), dma(2), dma(3),
         pltpu.SemaphoreType.DMA, dma(NY), dma(NY + 3), dma(NZ), dma(3),
         dma(NY), dma(3), dma(NY), dma(NY),
         dma(NZ), dma(3), dma(NY), dma(3),
         dma(NZ), dma(3), dma(NY), dma(3),
         dma(NX), dma(3), dma(NY), dma(NY),
-        dma(NX), dma(3), dma(NY), dma(3), dma(NZ), dma(3),
+        dma(NX), dma(3), dma(NY), dma(3), dma(2, NZ), dma(2, NZ),
         dma(NY), dma(3), dma(NZ), dma(3),
         dma(NY, NZ), dma(3, NZ),
+    ]
+    inputs = [
+        pltpu.with_memory_space_constraint(a, pltpu.HBM)
+        for a in (
+            activations[0], value_gradient[0], value_matrix[0], adapter_down_weight[0, 0], adapter_up_weight[0, 0]
+        )
     ]
     received, down_gradient, up_gradient = pl.pallas_call(
         kernel,
@@ -501,15 +578,11 @@
         out_specs=(vmem, vmem, vmem),
         scratch_shapes=scratch,
         compiler_params=pltpu.CompilerParams(
-            collective_id=0, has_side_effects=True, vmem_limit_bytes=63 << 20
+            collective_id=0, has_side_effects=True, vmem_limit_bytes=40 << 20
         ),
         name="relay_backward",
     )(
-        activations[0],
-        value_gradient[0],
-        value_matrix[0],
-        adapter_down_weight[0, 0],
-        adapter_up_weight[0, 0],
+        *inputs,
         segment_adapter[0],
         adapter_slot,
     )

time: 99.7 us -> 89.5 us (0.90)
  Pallas kernels: 95.1 us -> 85.8 us
    pallas_call x1, Pallas kernels: 95.1 us -> 85.8 us  [body(): pl.pallas_call(kernel, out_shape=(jax.ShapeDtypeStruct((rows, width), BF1...]
where the time goes in v3:
time: 89.5 us; the launch traced here: 89.4 us
  Pallas kernels  85.8 us (96%)
  local copies, waits for them, and re-layouts  2.89 us (3%)
    pallas_call x1, Pallas kernels, body(): pl.pallas_call(kernel, out_shape=(jax.ShapeDtypeStruct((rows, width), BF1...  85.8 us
    unnamed x7, local copies, waits for them, and re-layouts  2.89 us

profile of v3, /device:TPU:1, one launch (start us, length us, event | category | flops | bytes accessed | tf_op | source)
XLA Modules:
  0.0 89.4 jit_solution(6607282238535936066)
XLA Ops:
  0.6 0.0 copy-start
  0.6 0.0 copy-start.1
  0.7 0.6 copy-done
  1.3 0.0 copy-done.1
  1.3 85.8 %relay_backward.1 = (bf16[256,2048]{1,0:T(8,128)(2,1)S(1)}, bf16[32,2048]{1,0:T(8,128)(2,1)S(1)}, bf16[32,256]{1,0:T(8,128)(2,1)S(1)}) custom-call(bf16[256,2048]{1,0:T(8,128)(2,1)} %bitcast.13, bf16[256,256]{1,0:T(8,128)(2,1)} %bitcast.15, bf16[128,1024]{1,0:T(8,128)(2,1)} %bitcast.14, bf16[32,2048]{1,0:T(8,128)(2,1)} %bitcast.16, ...), custom_call_target="tpu_custom_call" | custom-call | tf_op jit(solution)/shard_map/relay_backward/pallas_call | solution.py:570
  87.2 1.0 %copy.13 = bf16[1,256,2048]{2,1,0:T(8,128)(2,1)} copy(bf16[1,256,2048]{2,1,0:T(8,128)(2,1)S(1)} %bitcast.9) | data formatting | bytes 2097152
  88.1 0.7 copy.14
  88.8 0.6 copy.15
Async XLA Ops:
  0.6 0.7 copy-start
  0.6 0.7 copy-start.1

commit v4 on v3

--- a/solution.py
+++ b/solution.py
@@ -118,16 +118,15 @@
         load.start()
 
     bar = pltpu.get_barrier_semaphore()
-    peers = (
+    senders = (
         [at(y_=p) for p in y_peers] + [at(x_=p) for p in x_peers] + [at(z_=p) for p in z_peers]
-        + [at(s_=before, y_=k) for k in range(NY)] + [at(s_=after, y_=k) for k in range(NY)]
-        + [at(s_=(s + 2) % NS), at(s_=(s + 6) % NS), at(s_=(s + 3 + 2 * (s % 2)) % NS)]
+        + [at(s_=after, y_=k) for k in range(NY)] + [at(s_=(s + 6 - s % 2) % NS)]
     )
-    for p in peers:
+    for p in senders:
         pl.semaphore_signal(bar, inc=1, device_id=p, device_id_type=MESH)
     si[y, 0:1, :] = jnp.full((1, 128), slot[seg[0]], jnp.int32)
     si[y, 1:2, :] = jnp.full((1, 128), slot[seg[1]], jnp.int32)
-    pl.semaphore_wait(bar, len(peers))
+    pl.semaphore_wait(bar, 9 + NY + 2 * (1 - s % 2))
 
     def g_block(x_, y_):
         return gf.at[x_, block(y_, rows)]
@@ -401,13 +400,10 @@
     def product(i):
         place = block(y * NZ + i, chunk)
 
-        @pl.loop(0, NY)
-        def _(p):
-            r = block(p, rows)
-            total = nn_dot(rx[r, :], dn[:, :, block(i, chunk)].reshape(slots_wide, chunk))
-            for q in range(NX):
-                total += nt_dot(gf[q, r, :], wn[i, :, q * rows:(q + 1) * rows])
-            ot[i, r, :] = total.astype(BF16)
+        total = nn_dot(rx[...], dn[:, :, block(i, chunk)].reshape(slots_wide, chunk))
+        for q in range(NX):
+            total += nt_dot(gf[q], wn[i, :, q * rows:(q + 1) * rows])
+        ot[i] = total.astype(BF16)
 
         for k, p in enumerate(y_peers):
             copy(ot.at[i, block(p, rows)], out.at[:, place], o_s.at[k, i], o_r.at[y, i], at(y_=p)).start()
@@ -448,42 +444,34 @@
     def w_step2():
         w_step(2)
 
-    on(1, slots_out, up_out, g_shift)
-    on(0, slots_out)
-    on(1, slots_next_out)
-    on(0, g_shift)
-    on(1, w_shift)
-    on(0, far0, up_out, far1, g_start_y)
-    on(None, picks)
-    on(0, w_start, slots_next_out)
-    on(1, down_out)
-    on(None, up_pick)
-    on(0, down_out)
-    on(None, rank_part, rank_sum, down_part)
-    on(0, g_start_x, w_shift)
-    on(1, g_start_y)
-    on(0, down_wait, g_relay)
-    on(1, down_wait)
+    on(None, slots_out, up_out, w_shift, g_shift)
+    on(0, far0, w_start)
+    on(None, down_out)
+    on(None, picks, up_pick)
+    on(0, g_start_y, far1)
+    on(None, rank_part)
+    on(0, g_start_x)
+    on(None, rank_sum, down_part, slots_next_out)
+    on(0, g_relay)
+    on(1, w_start)
+    on(0, w_step1, far2)
+    on(1, g_start_y, g_start_x)
+    on(None, down_wait)
     on(None, down_pick)
-    on(0, w_step1)
-    on(1, g_start_x)
-    on(0, far2)
-    on(1, g_relay, dn_start, w_start, down_next)
+    on(1, down_next)
+    on(1, w_step1)
+    on(0, w_step2, rank_spread)
+    on(1, g_relay)
     on(None, down_sum)
-    on(1, rank_spread)
-    on(0, w_step2, rank_spread, g_wait, dn_wait0)
-    on(1, w_step1)
-    on(0, product0, product1)
-    on(None, hidden_part)
+    on(1, dn_start, w_step2, rank_spread)
+    on(None, down_hop1, hidden_part)
     on(1, dn_relay)
-    on(0, product2)
-    on(1, w_step2, g_wait, dn_wait1)
-    on(None, down_hop1, up_part)
-    on(1, product0, product1)
+    on(0, dn_wait0, g_wait, product0, product1, product2)
+    on(None, down_hop2, up_part)
+    on(1, dn_wait1, g_wait)
     on(0, product3)
-    on(None, down_hop2)
-    on(1, product2, product3)
-    on(None, up_sum, up_end, down_end, out_end)
+    on(1, product0, product1, product2, product3)
+    on(None, up_sum, down_end, up_end, out_end)
 
     for core in (None, 0, 1):
         group = [e[1:] for e in started if e[0] == core]

time: 89.5 us -> 87.7 us (0.980)
  Pallas kernels: 85.8 us -> 84 us
    pallas_call x1, Pallas kernels: 85.8 us -> 84 us  [body(): pl.pallas_call(kernel, out_shape=(jax.ShapeDtypeStruct((rows, width), BF1...]
where the time goes in v4:
time: 87.7 us; the launch traced here: 87.6 us
  Pallas kernels  84 us (96%)
  local copies, waits for them, and re-layouts  2.89 us (3%)
    pallas_call x1, Pallas kernels, body(): pl.pallas_call(kernel, out_shape=(jax.ShapeDtypeStruct((rows, width), BF1...  84 us
    unnamed x7, local copies, waits for them, and re-layouts  2.89 us

profile of v4, /device:TPU:1, one launch (start us, length us, event | category | flops | bytes accessed | tf_op | source)
XLA Modules:
  0.0 87.6 jit_solution(7937392537621670236)
XLA Ops:
  0.6 0.0 copy-start
  0.6 0.0 copy-start.1
  0.7 0.6 copy-done
  1.3 0.0 copy-done.1
  1.3 84.0 %relay_backward.1 = (bf16[256,2048]{1,0:T(8,128)(2,1)S(1)}, bf16[32,2048]{1,0:T(8,128)(2,1)S(1)}, bf16[32,256]{1,0:T(8,128)(2,1)S(1)}) custom-call(bf16[256,2048]{1,0:T(8,128)(2,1)} %bitcast.13, bf16[256,256]{1,0:T(8,128)(2,1)} %bitcast.15, bf16[128,1024]{1,0:T(8,128)(2,1)} %bitcast.14, bf16[32,2048]{1,0:T(8,128)(2,1)} %bitcast.16, ...), custom_call_target="tpu_custom_call" | custom-call | tf_op jit(solution)/shard_map/relay_backward/pallas_call | solution.py:558
  85.3 1.0 %copy.13 = bf16[1,256,2048]{2,1,0:T(8,128)(2,1)} copy(bf16[1,256,2048]{2,1,0:T(8,128)(2,1)S(1)} %bitcast.9) | data formatting | bytes 2097152
  86.3 0.7 copy.14
  87.0 0.6 copy.15
Async XLA Ops:
  0.6 0.7 copy-start
  0.6 0.7 copy-start.1

commit v5 on v4

--- a/solution.py
+++ b/solution.py
@@ -460,15 +460,15 @@
     on(None, down_pick)
     on(1, down_next)
     on(1, w_step1)
-    on(0, w_step2, rank_spread)
+    on(0, w_step2)
     on(1, g_relay)
     on(None, down_sum)
-    on(1, dn_start, w_step2, rank_spread)
+    on(1, dn_start, w_step2)
     on(None, down_hop1, hidden_part)
     on(1, dn_relay)
-    on(0, dn_wait0, g_wait, product0, product1, product2)
+    on(0, rank_spread, dn_wait0, g_wait, product0, product1, product2)
     on(None, down_hop2, up_part)
-    on(1, dn_wait1, g_wait)
+    on(1, rank_spread, dn_wait1, g_wait)
     on(0, product3)
     on(1, product0, product1, product2, product3)
     on(None, up_sum, down_end, up_end, out_end)

time: 87.7 us -> 87.3 us (level)
  no operation moved by 1% of the time
where the time goes in v5:
time: 87.3 us; the launch traced here: 87.1 us
  Pallas kernels  83.6 us (96%)
  local copies, waits for them, and re-layouts  2.89 us (3%)
    pallas_call x1, Pallas kernels, body(): pl.pallas_call(kernel, out_shape=(jax.ShapeDtypeStruct((rows, width), BF1...  83.6 us
    unnamed x7, local copies, waits for them, and re-layouts  2.89 us

profile of v5, /device:TPU:1, one launch (start us, length us, event | category | flops | bytes accessed | tf_op | source)
XLA Modules:
  0.0 87.1 jit_solution(9447751672038432695)
XLA Ops:
  0.6 0.0 copy-start
  0.6 0.0 copy-start.1
  0.7 0.6 copy-done
  1.3 0.0 copy-done.1
  1.3 83.6 %relay_backward.1 = (bf16[256,2048]{1,0:T(8,128)(2,1)S(1)}, bf16[32,2048]{1,0:T(8,128)(2,1)S(1)}, bf16[32,256]{1,0:T(8,128)(2,1)S(1)}) custom-call(bf16[256,2048]{1,0:T(8,128)(2,1)} %bitcast.13, bf16[256,256]{1,0:T(8,128)(2,1)} %bitcast.15, bf16[128,1024]{1,0:T(8,128)(2,1)} %bitcast.14, bf16[32,2048]{1,0:T(8,128)(2,1)} %bitcast.16, ...), custom_call_target="tpu_custom_call" | custom-call | tf_op jit(solution)/shard_map/relay_backward/pallas_call | solution.py:558
  84.9 1.0 %copy.13 = bf16[1,256,2048]{2,1,0:T(8,128)(2,1)} copy(bf16[1,256,2048]{2,1,0:T(8,128)(2,1)S(1)} %bitcast.9) | data formatting | bytes 2097152
  85.9 0.7 copy.14
  86.5 0.6 copy.15
Async XLA Ops:
  0.6 0.7 copy-start
  0.6 0.7 copy-start.1
